TPU v7x, 32 devices: a whole 2x2x4 slice. The times are simulated.
32 devices in a mesh: rep: 2 (over y), grp: 4 (over z), img: 4 (over x, core).
Axes of the slice: x: 2, y: 2, z: 4, core: 2. Of those that a mesh axis runs over, the one named last changes fastest.
Arguments:
- patches: bfloat16 [4, 512, 2560], P('grp', 'rep'), parts along dimension 1, may hold values from -6 to 6
- embed_kernel: bfloat16 [4, 2560, 1024], P('grp', None, 'img'), may hold values from -0.125 to 0.125
- location_embed: bfloat16 [64, 1024], P(None, 'img'), may hold values from -3 to 3
- attn_in: bfloat16 [2, 1024, 3, 1024], P(None, 'grp', None, 'img'), may hold values from -0.25 to 0.25
- attn_out: bfloat16 [2, 1024, 1024], P(None, 'img', 'grp'), may hold values from -0.1875 to 0.1875
- ffn_up: bfloat16 [1024, 4096], P('grp', 'img'), may hold values from -0.1875 to 0.1875
- ffn_down: bfloat16 [4096, 1024], P('img', 'grp'), may hold values from -0.09375 to 0.09375
- head_kernel: bfloat16 [4, 1024, 2560], P('grp', None, 'img'), may hold values from -0.1875 to 0.1875
Outputs:
- recon: bfloat16 [4, 512, 2560], P('grp', 'rep', 'img'), parts along dimension 1
There are 2 independent parts, one for each index of `rep`. A program takes and returns all parts, laid end to end along the dimension named above; an argument that names none is the same for every part. Nothing has to cross between parts.
All inputs are finite; a program needn't handle non-finite values.
Results may differ from a plain program's by a relative error of at most 0.02.
Values may be sent and summed in bfloat16 or wider, within the bound.
A program may use at most 64 MiB of HBM per device.

v0:
```python
import jax
import jax.numpy as jnp
from jax import lax
from jax.sharding import PartitionSpec as P

HD = 64


def norm_rows(stream):
    values = stream.astype(jnp.float32)
    center = values - jnp.mean(values, axis=-1, keepdims=True)
    spread = jnp.mean(center * center, axis=-1, keepdims=True)
    return (center * lax.rsqrt(spread + 1e-05)).astype(jnp.bfloat16)


def attend(query, keys, values, layout, form_scores, form_out):
    tokens, width = query.shape
    heads = width // HD
    shape = layout + (heads, HD)
    scores = jnp.einsum(
        form_scores, query.reshape(shape), keys.reshape(shape), preferred_element_type=jnp.float32
    )
    scores = scores * HD ** (-0.5)
    top = jnp.max(scores, axis=-1, keepdims=True)
    expo = jnp.exp(scores - top)
    probs = (expo / jnp.sum(expo, axis=-1, keepdims=True)).astype(jnp.bfloat16)
    mixed = jnp.einsum(form_out, probs, values.reshape(shape), preferred_element_type=jnp.float32)
    return mixed.astype(jnp.bfloat16).reshape(tokens, width)


def widen(stream):
    return lax.all_gather(stream, "img", axis=1, tiled=True)


def add_branch(stream, branch):
    total = lax.psum(branch.astype(jnp.bfloat16), "img").astype(jnp.float32)
    return (stream.astype(jnp.float32) + total).astype(jnp.bfloat16)


def block(stream, w_in, w_out, layout, form_scores, form_out):
    normed = norm_rows(stream)
    model_width, triple, local_width = w_in.shape
    qkv = jnp.dot(
        normed, w_in.reshape(model_width, triple * local_width), preferred_element_type=jnp.float32
    )
    qkv = qkv.astype(jnp.bfloat16).reshape(-1, triple, local_width)
    mixed = attend(qkv[:, 0], qkv[:, 1], qkv[:, 2], layout, form_scores, form_out)
    branch = jnp.dot(mixed, w_out, preferred_element_type=jnp.float32)
    return add_branch(stream, branch)


def feed_forward(stream, w_up, w_down):
    normed = norm_rows(stream)
    inner = jax.nn.gelu(
        jnp.dot(normed, w_up, preferred_element_type=jnp.float32), approximate=False
    )
    inner = inner.astype(jnp.bfloat16)
    branch = jnp.dot(inner, w_down, preferred_element_type=jnp.float32)
    return add_branch(stream, branch)


def local(patches, embed_kernel, location_embed, attn_in, attn_out, ffn_up, ffn_down, head_kernel):
    loc_count = location_embed.shape[0]
    rows = patches.shape[1]
    images = rows // loc_count
    groups = lax.axis_size("grp")
    per_group = rows // groups

    def fetch(index):
        return (
            lax.all_gather(attn_in[index], "grp", axis=0, tiled=True),
            lax.all_gather(attn_out[index], "grp", axis=1, tiled=True),
        )

    hidden = jax.nn.gelu(
        jnp.dot(patches[0], embed_kernel[0], preferred_element_type=jnp.float32), approximate=False
    )
    share = (hidden.reshape(images, loc_count, -1) + location_embed.astype(jnp.float32)).astype(
        jnp.bfloat16
    )
    share = share.reshape(rows, -1)
    stream = widen(share)
    width = stream.shape[1]
    w_in, w_out = fetch(0)
    stream = block(stream, w_in, w_out, (images, loc_count), "ilhe,imhe->ihlm", "ihlm,imhe->ilhe")
    placed = lax.all_to_all(
        stream.reshape(1, rows, width), "grp", split_axis=1, concat_axis=0, tiled=True
    )
    placed = placed.reshape(groups * per_group, width)
    w_in, w_out = fetch(1)
    placed = block(placed, w_in, w_out, (groups, per_group), "gmhe,kmhe->mhgk", "mhgk,kmhe->gmhe")
    w_up, w_down = (
        lax.all_gather(ffn_up, "grp", axis=0, tiled=True),
        lax.all_gather(ffn_down, "grp", axis=1, tiled=True),
    )
    placed = feed_forward(placed, w_up, w_down)
    returned = lax.all_to_all(
        placed.reshape(groups, per_group, width), "grp", split_axis=0, concat_axis=1, tiled=True
    )
    final = returned.reshape(rows, width)
    recon = jnp.dot(final, head_kernel[0], preferred_element_type=jnp.float32).astype(jnp.bfloat16)
    return recon[None]


def solution(mesh):
    return jax.shard_map(
        local,
        mesh=mesh,
        in_specs=(
            P("grp", "rep", None),
            P("grp", None, "img"),
            P(None, "img"),
            P(None, "grp", None, "img"),
            P(None, "img", "grp"),
            P("grp", "img"),
            P("img", "grp"),
            P("grp", None, "img"),
        ),
        out_specs=P("grp", "rep", "img"),
        check_vma=False,
    )
```

profile of v0, /device:TPU:1, one launch (start us, length us, event | category | flops | bytes accessed | tf_op | source)
XLA Modules:
  0.0 356.5 jit_solution(12065482046709374442)
XLA Ops:
  6.5 1.3 fusion.155
  8.9 2.4 fusion.99
  11.3 8.5 %all_gather.21 = bf16[256,1024]{1,0:T(8,128)(2,1)S(1)} all-gather(bf16[256,256]{1,0:T(8,128)(2,1)S(1)} %fusion.99), channel_id=1, replica_groups=mesh['rep'=2,'grp'=4,'img'=4] {'img'}, dimensions={1}, use_global_device_ids=true | all-gather | bytes 655360 | tf_op jit(solution)/shard_map/all_gather | solution.py:32
  20.3 21.2 %all-gather.1 = bf16[1,256,1024]{2,1,0:T(8,128)(2,1)S(1)} all-gather(bf16[1,256,256]{2,1,0:T(8,128)(2,1)S(1)} %get-tuple-element.18), channel_id=3, replica_groups=mesh['rep'=2,'grp'=4,'img'=4] {'grp'}, dimensions={2}, use_global_device_ids=true | all-gather | bytes 655360 | tf_op jit(solution)/shard_map/all_gather | solution.py:72
  41.5 17.5 %all-gather.13.cloned.1.call-done = bf16[1,1024,3,256]{1,3,2,0:T(8,128)(2,1)} async-done(((bf16[1,256,3,256]{1,3,2,0:T(8,128)(2,1)}), bf16[1,1024,3,256]{1,3,2,0:T(8,128)(2,1)}) %all-gather.13.cloned.1.call-update) | async-done | bytes 1572880 | tf_op jit(solution)/shard_map/all_gather | solution.py:71
  59.0 2.8 convolution_convert_fusion.4
  61.8 1.2 copy.32
  63.8 1.1 reshape.158
  64.9 1.1 convolution_multiply_fusion.1
  66.5 1.5 fusion.23
  68.4 1.1 convolution_convert_fusion.1
  69.6 0.9 copy.68
  70.5 27.2 %all-reduce.4.cloned.1.call-done = bf16[256,1024]{1,0:T(8,128)(2,1)} async-done(((bf16[256,1024]{1,0:T(8,128)(2,1)}), bf16[256,1024]{1,0:T(8,128)(2,1)}) %all-reduce.4.cloned.1.call-update) | async-done | bytes 524304 | tf_op jit(solution)/shard_map/psum | solution.py:36
  97.7 1.2 fusion.46
  100.3 3.7 %reduce.4 = bf16[256,1024]{1,0:T(8,128)(2,1)S(1)} reduce(bf16[256,1,1024]{2,1,0:T(2,128)(2,1)S(1)} %bitcast.76, bf16[]{:T(256)} %broadcast.113), dimensions={1}, to_apply=%bitcast.75.reduce_sub_computation | reduce | bytes 1048578
  104.0 1.2 reshape.162
  105.2 4.9 %all-to-all-start = ((bf16[4,2,32768]{2,1,0:T(2,128)(2,1)}), bf16[4,2,32768]{2,1,0:T(2,128)(2,1)S(1)}, u32[]{:S(2)}, u32[]{:S(2)}) async-start(bf16[4,2,32768]{2,1,0:T(2,128)(2,1)} %reshape.162), calls=%async_computation | async-start | bytes 1048576 | tf_op jit(solution)/shard_map/all_to_all | solution.py:86
  110.1 44.2 %all-gather.3 = bf16[1,256,1024]{2,1,0:T(8,128)(2,1)} all-gather(bf16[1,256,256]{2,1,0:T(8,128)(2,1)S(1)} %get-tuple-element.17), channel_id=5, replica_groups=mesh['rep'=2,'grp'=4,'img'=4] {'grp'}, dimensions={2}, use_global_device_ids=true | all-gather | bytes 655360 | tf_op jit(solution)/shard_map/all_gather | solution.py:72
  155.4 2.2 all-gather.15.cloned.1.call-done
  157.6 2.0 convolution_convert_fusion.3
  161.2 1.7 fusion.164
  163.0 1.6 fusion.24
  164.9 1.1 convolution_convert_fusion
  167.3 29.6 %all-reduce.6.cloned.1.call-done = bf16[256,1024]{1,0:T(8,128)(2,1)} async-done(((bf16[256,1024]{1,0:T(8,128)(2,1)}), bf16[256,1024]{1,0:T(8,128)(2,1)}) %all-reduce.6.cloned.1.call-update) | async-done | bytes 524304 | tf_op jit(solution)/shard_map/psum | solution.py:36
  196.9 1.3 convert_reduce_fusion.1
  198.5 46.9 %all-gather.11.cloned.1.call-done = bf16[1024,1024]{1,0:T(8,128)(2,1)} async-done(((bf16[1024,256]{1,0:T(8,128)(2,1)}), bf16[1024,1024]{1,0:T(8,128)(2,1)}) %all-gather.11.cloned.1.call-update) | async-done | bytes 2097168 | tf_op jit(solution)/shard_map/all_gather | solution.py:94
  245.4 46.3 %all-gather.9.cloned.1.call-done = bf16[1024,1024]{1,0:T(8,128)(2,1)} async-done(((bf16[256,1024]{1,0:T(8,128)(2,1)}), bf16[1024,1024]{1,0:T(8,128)(2,1)}) %all-gather.9.cloned.1.call-update) | async-done | bytes 2097168 | tf_op jit(solution)/shard_map/all_gather | solution.py:93
  291.7 6.6 %convolution_convert_fusion.2 = bf16[256,1024]{1,0:T(8,128)(2,1)} fusion(bf16[1024,1024]{1,0:T(8,128)(2,1)} %all-gather.11.cloned.1.call-done, bf16[1024,1024]{1,0:T(8,128)(2,1)} %all-gather.9.cloned.1.call-done, bf16[256,1024]{1,0:T(8,128)(2,1)S(1)} %get-tuple-element.6, f32[256]{0:T(256)S(1)} %add_rsqrt_fusion, f32[256]{0:T(256)S(1)} %broadcast_multiply_fusion), kind=kOutput, calls=%fused_computation.19 | convolution fusion | flops 1092091904 | bytes 5244928 | tf_op jit(solution)/shard_map/dot_general | solution.py:58
  298.3 30.5 %all-reduce.8.cloned.1.call-done = bf16[256,1024]{1,0:T(8,128)(2,1)} async-done(((bf16[256,1024]{1,0:T(8,128)(2,1)}), bf16[256,1024]{1,0:T(8,128)(2,1)}) %all-reduce.8.cloned.1.call-update) | async-done | bytes 524304 | tf_op jit(solution)/shard_map/psum | solution.py:36
  328.8 1.2 fusion.32
  330.1 18.3 %all_to_all.8 = bf16[4,64,1024]{2,1,0:T(8,128)(2,1)S(1)} all-to-all(bf16[4,64,1024]{2,1,0:T(8,128)(2,1)S(1)} %bitcast.78), channel_id=1, replica_groups=mesh['rep'=2,'grp'=4,'img'=4] {'grp'}, dimensions={0} | all-to-all | bytes 1048576 | tf_op jit(solution)/shard_map/all_to_all | solution.py:97
  348.3 1.3 fusion.20
  (58 shorter events, 9.0 us)
Async XLA Ops:
  6.5 341.8 %copy-start = (bf16[1,1024,640]{2,1,0:T(8,128)(2,1)S(1)}, bf16[1,1024,640]{2,1,0:T(8,128)(2,1)}, u32[]{:S(2)}) copy-start(bf16[1,1024,640]{2,1,0:T(8,128)(2,1)} %param.15) | copy-start | bytes 3932164
  6.5 2.3 copy-start.4
  6.5 2.3 copy-start.2
  6.5 52.4 %all-gather.13.cloned.1.call-start = ((), (), s32[]{:S(2)}) async-start(), calls=%async_computation.7 | async-start | bytes 1966080 | tf_op jit(solution)/shard_map/all_gather | solution.py:71
  8.8 88.9 %all-reduce.4.cloned.1.call-start = ((), (), s32[]{:S(2)}) async-start(), calls=%async_computation.2 | async-start | bytes 1048576 | tf_op jit(solution)/shard_map/psum | solution.py:36
  8.9 11.4 %copy-start.3 = (bf16[2,256,256]{2,1,0:T(8,128)(2,1)S(1)}, bf16[2,256,256]{2,1,0:T(8,128)(2,1)}, u32[]{:S(2)}) copy-start(bf16[2,256,256]{2,1,0:T(8,128)(2,1)} %param.12) | copy-start | bytes 786436
  69.5 88.1 %all-gather.15.cloned.1.call-start = ((), (), s32[]{:S(2)}) async-start(), calls=%async_computation.8 | async-start | bytes 1966080 | tf_op jit(solution)/shard_map/all_gather | solution.py:71
  105.2 49.1 %all-to-all-start = ((bf16[4,2,32768]{2,1,0:T(2,128)(2,1)}), bf16[4,2,32768]{2,1,0:T(2,128)(2,1)S(1)}, u32[]{:S(2)}, u32[]{:S(2)}) async-start(bf16[4,2,32768]{2,1,0:T(2,128)(2,1)} %reshape.162), calls=%async_computation | async-start | bytes 1048576 | tf_op jit(solution)/shard_map/all_to_all | solution.py:86
  110.1 86.8 %all-reduce.6.cloned.1.call-start = ((), (), s32[]{:S(2)}) async-start(), calls=%async_computation.3 | async-start | bytes 1048576 | tf_op jit(solution)/shard_map/psum | solution.py:36
  162.9 1.9 copy-start.1
  166.0 79.3 %all-gather.11.cloned.1.call-start = ((), (), s32[]{:S(2)}) async-start(), calls=%async_computation.5 | async-start | bytes 2621440 | tf_op jit(solution)/shard_map/all_gather | solution.py:94
  166.6 125.1 %all-gather.9.cloned.1.call-start = ((), (), s32[]{:S(2)}) async-start(), calls=%async_computation.4 | async-start | bytes 2621440 | tf_op jit(solution)/shard_map/all_gather | solution.py:93
  167.2 161.6 %all-reduce.8.cloned.1.call-start = ((), (), s32[]{:S(2)}) async-start(), calls=%async_computation.6 | async-start | bytes 1048576 | tf_op jit(solution)/shard_map/psum | solution.py:36
Sparse Core Ops, SparseCore 0:
  8.9 50.0 all-gather.12
  69.7 28.0 all-reduce.3
  99.3 58.2 all-gather.14
  166.2 30.6 all-reduce.5
  198.3 47.0 all-gather.10
  246.8 44.8 all-gather.8
  298.4 30.3 all-reduce.7
where the time goes:
time: 359 us; the launch traced here: 356 us
  waiting for transfers between devices  201 us (56%)
  blocking collectives  92.2 us (26%)
  matrix products  23.6 us (7%)
  between operations  13.8 us (4%)
  local copies, waits for them, and re-layouts  11.7 us (3%)
  other arithmetic  8.73 us (2%)
  starting transfers between devices  5.07 us (1%)
    psum x3, waiting for transfers between devices, add_branch(): total = lax.psum(branch.astype(jnp.bfloat16), 'img').astype(jnp.float32)  87.4 us
    all_gather x2, blocking collectives, fetch(): lax.all_gather(attn_out[index], 'grp', axis=1, tiled=True)  65.5 us
    all_gather x1, waiting for transfers between devices, local(): lax.all_gather(ffn_down, 'grp', axis=1, tiled=True)  46.9 us
    all_gather x1, waiting for transfers between devices, local(): lax.all_gather(ffn_up, 'grp', axis=0, tiled=True)  46.3 us
    all_gather x2, waiting for transfers between devices, fetch(): lax.all_gather(attn_in[index], 'grp', axis=0, tiled=True)  19.7 us
    all_to_all x1, blocking collectives, local(): lax.all_to_all(placed.reshape(groups, per_group, width), 'grp', split_axi...  18.3 us
    all_gather x1, blocking collectives, widen(): return lax.all_gather(stream, 'img', axis=1, tiled=True)  8.51 us
  transfers between devices with their start and end apart: 8, of which 7 were waited for; matrix products, arithmetic and copies ran while one was open for 4% of the time, Pallas kernels for 0%

commit v1 on v0

--- a/solution.py
+++ b/solution.py
@@ -1,9 +1,15 @@
+import functools
+import math
+
 import jax
 import jax.numpy as jnp
 from jax import lax
+from jax.experimental import pallas as pl
+from jax.experimental.pallas import tpu as pltpu
 from jax.sharding import PartitionSpec as P
 
 HD = 64
+MESH = pl.DeviceIdType.MESH
 
 
 def norm_rows(stream):
@@ -102,9 +108,330 @@
     return recon[None]
 
 
+def gelu_exact(x):
+    return 0.5 * x * (1.0 + lax.erf(x * math.sqrt(0.5)))
+
+
+def mm(a, b):
+    return jnp.dot(a, b, preferred_element_type=jnp.float32)
+
+
+def normalise(values):
+    center = values - jnp.mean(values, axis=-1, keepdims=True)
+    spread = jnp.mean(center * center, axis=-1, keepdims=True)
+    return (center * lax.rsqrt(spread + 1e-05)).astype(jnp.bfloat16)
+
+
+def head_attention(query, keys, values, mask):
+    tokens, width = query.shape
+    lane_head = lax.broadcasted_iota(jnp.int32, (tokens, width), 1) // HD
+    mixed = jnp.zeros((tokens, width), jnp.float32)
+    for head in range(width // HD):
+        here = lane_head == head
+        own = jnp.where(here, query, 0.0).astype(jnp.bfloat16)
+        scores = lax.dot_general(
+            own, keys, (((1,), (1,)), ((), ())), preferred_element_type=jnp.float32
+        ) * HD ** (-0.5)
+        scores = jnp.where(mask, scores, -jnp.inf)
+        top = jnp.max(scores, axis=-1, keepdims=True)
+        expo = jnp.exp(scores - top)
+        probs = (expo / jnp.sum(expo, axis=-1, keepdims=True)).astype(jnp.bfloat16)
+        mixed = jnp.where(here, mm(probs, values), mixed)
+    return mixed.astype(jnp.bfloat16)
+
+
+def fused(
+    dims,
+    patches, embed, loc_in, w_in0, w_in1, w_out, up, down, head,
+    out,
+    patches_v, embed_v, loc_v, head_v,
+    win0, win1, wout0, wout1, up_v, down_v,
+    feats, nrm0, nrm1, nrm2, part, rs, keep, a2a, back, fin, hid,
+    zsend, zrecv, ysend, yrecv, xsend, xrecv, tsend, trecv, lsem, barrier_pad,
+):
+    n_rep, n_grp, n_img, rows, width = dims
+    own = rows // n_img
+    loc = own // n_grp
+    y = lax.axis_index("rep")
+    g = lax.axis_index("grp")
+    i = lax.axis_index("img")
+
+    def peer(me, n, d):
+        return lax.rem(me + d, n)
+
+    barrier = pltpu.get_barrier_semaphore()
+    for axis, me, n in (("grp", g, n_grp), ("img", i, n_img), ("rep", y, n_rep)):
+        for d in range(1, n):
+            pl.semaphore_signal(
+                barrier, inc=1, device_id={axis: peer(me, n, d)}, device_id_type=MESH
+            )
+
+    started = []
+
+    def remote(src, dst, send, recv, axis, to):
+        copy = pltpu.make_async_remote_copy(
+            src_ref=src, dst_ref=dst, send_sem=send, recv_sem=recv,
+            device_id={axis: to}, device_id_type=MESH,
+        )
+        copy.start()
+        started.append(copy)
+
+    def arrived(dst, send, recv, axis, to):
+        pltpu.make_async_remote_copy(
+            src_ref=dst, dst_ref=dst, send_sem=send, recv_sem=recv,
+            device_id={axis: to}, device_id_type=MESH,
+        ).wait_recv()
+
+    def cut1(ref, half):
+        size = ref.shape[0] // n_rep
+        return ref.at[pl.ds(pl.multiple_of(half * size, size), size)]
+
+    def cut2(ref, half):
+        size = ref.shape[1] // n_rep
+        return ref.at[:, pl.ds(pl.multiple_of(half * size, size), size)]
+
+    weights = (
+        (w_in0, win0, cut2),
+        (w_out.at[0], wout0, cut1),
+        (w_in1, win1, cut2),
+        (w_out.at[1], wout1, cut1),
+        (up, up_v, cut1),
+        (down, down_v, cut1),
+    )
+    locals_ = []
+
+    def local_copy(src, dst):
+        copy = pltpu.make_async_copy(src, dst, lsem.at[len(locals_)])
+        copy.start()
+        locals_.append(copy)
+        return copy
+
+    def start_z(k):
+        shard, full, cut = weights[k]
+        for d in range(1, n_grp):
+            remote(
+                cut(shard, y), cut(full.at[g], y),
+                zsend.at[k, d], zrecv.at[k, g], "grp", peer(g, n_grp, d),
+            )
+
+    def forward(k, hops=None):
+        shard, full, cut = weights[k]
+        for d in hops or range(1, n_grp):
+            src = peer(g, n_grp, d)
+            arrived(cut(full.at[src], y), zsend.at[k, d], zrecv.at[k, src], "grp", src)
+            remote(
+                cut(full.at[src], y), cut(full.at[src], y),
+                ysend.at[k, d], yrecv.at[k, src], "rep", peer(y, n_rep, 1),
+            )
+
+    def ready(k):
+        shard, full, cut = weights[k]
+        for d in range(1, n_grp):
+            src = peer(g, n_grp, d)
+            half = peer(y, n_rep, 1)
+            arrived(cut(full.at[src], half), ysend.at[k, d], yrecv.at[k, src], "rep", half)
+        own_copies[k].wait()
+
+    def spread(k, src_of, dst):
+        for d in range(1, n_img):
+            to = peer(i, n_img, d)
+            remote(src_of(to), dst.at[i], xsend.at[k, d], xrecv.at[k, i], "img", to)
+
+    def collected(k, dst):
+        for d in range(1, n_img):
+            src = peer(i, n_img, d)
+            arrived(dst.at[src], xsend.at[k, d], xrecv.at[k, src], "img", src)
+
+    in_copies = [
+        local_copy(patches.at[0], patches_v),
+        local_copy(embed.at[0], embed_v),
+        local_copy(loc_in, loc_v),
+    ]
+    pl.semaphore_wait(barrier, n_grp + n_img + n_rep - 3)
+    start_z(0)
+    start_z(1)
+    own_copies = [local_copy(shard, full.at[g]) for shard, full, cut in weights]
+    head_copy = local_copy(head.at[0], head_v)
+
+    for copy in in_copies:
+        copy.wait()
+    hidden = gelu_exact(mm(patches_v[...], embed_v[...]))
+    places = loc_v[...].astype(jnp.float32)
+    images = rows // places.shape[0]
+    hidden = hidden.reshape(images, places.shape[0], hidden.shape[1]) + places[None]
+    feats[i] = hidden.reshape(rows, hidden.shape[2]).astype(jnp.bfloat16)
+    spread(0, lambda to: feats.at[i], feats)
+    start_z(2)
+    collected(0, feats)
+
+    chunk = width // n_img
+    chunks = [feats[s].astype(jnp.float32) for s in range(n_img)]
+    mean = sum(jnp.sum(c, axis=-1, keepdims=True) for c in chunks) / width
+    chunks = [c - mean for c in chunks]
+    spread_ = sum(jnp.sum(c * c, axis=-1, keepdims=True) for c in chunks) / width
+    scale = lax.rsqrt(spread_ + 1e-05)
+    for s in range(n_img):
+        nrm0[:, s * chunk:(s + 1) * chunk] = (chunks[s] * scale).astype(jnp.bfloat16)
+    mine = pl.ds(pl.multiple_of(i * own, own), own)
+    for s in range(n_img):
+        keep[0, :, s * chunk:(s + 1) * chunk] = feats[s, mine, :]
+    forward(0)
+    start_z(3)
+    forward(1)
+    start_z(4)
+
+    row_at = lax.broadcasted_iota(jnp.int32, (rows, rows), 0)
+    col_at = lax.broadcasted_iota(jnp.int32, (rows, rows), 1)
+    same_image = row_at // own == col_at // own
+    same_place = jnp.logical_and(same_image, row_at % loc == col_at % loc)
+
+    def project(normed, full):
+        depth = width // n_grp
+        total = None
+        for s in range(n_grp):
+            piece = normed[:, s * depth:(s + 1) * depth]
+            terms = [mm(piece, full[s, p]) for p in range(3)]
+            total = terms if total is None else [a + b for a, b in zip(total, terms)]
+        return [t.astype(jnp.bfloat16) for t in total]
+
+    def branch_out(k, mixed, full):
+        wide = width // n_grp
+        for s in range(n_grp):
+            part[k, :, s * wide:(s + 1) * wide] = mm(mixed, full[s]).astype(jnp.bfloat16)
+        spread(
+            1 + 2 * k,
+            lambda to: part.at[k, pl.ds(pl.multiple_of(to * own, own), own)],
+            rs.at[k],
+        )
+
+    def summed(k, stream):
+        total = part[k, mine, :].astype(jnp.float32)
+        collected(1 + 2 * k, rs.at[k])
+        for d in range(1, n_img):
+            total = total + rs[k, peer(i, n_img, d)].astype(jnp.float32)
+        return (stream.astype(jnp.float32) + total).astype(jnp.bfloat16)
+
+    ready(0)
+    query, keys, values = project(nrm0[...], win0)
+    mixed = head_attention(query, keys, values, same_image)
+    ready(1)
+    branch_out(0, mixed, wout0)
+    keep[1] = summed(0, keep[0])
+
+    for d in range(1, n_grp):
+        to = peer(g, n_grp, d)
+        remote(
+            keep.at[1, pl.ds(pl.multiple_of(to * loc, loc), loc)], a2a.at[g],
+            tsend.at[0, d], trecv.at[0, g], "grp", to,
+        )
+    a2a[g] = keep[1, pl.ds(pl.multiple_of(g * loc, loc), loc), :]
+    start_z(5)
+    for d in range(1, n_grp):
+        src = peer(g, n_grp, d)
+        arrived(a2a.at[src], tsend.at[0, d], trecv.at[0, src], "grp", src)
+    stream = a2a[...].reshape(own, width)
+    nrm1[i] = normalise(stream.astype(jnp.float32))
+    spread(2, lambda to: nrm1.at[i], nrm1)
+    forward(2)
+    forward(3)
+    collected(2, nrm1)
+
+    ready(2)
+    query, keys, values = project(nrm1[...].reshape(rows, width), win1)
+    mixed = head_attention(query, keys, values, same_place)
+    ready(3)
+    branch_out(1, mixed, wout1)
+    stream = summed(1, stream)
+    nrm2[i] = normalise(stream.astype(jnp.float32))
+    spread(4, lambda to: nrm2.at[i], nrm2)
+    forward(4)
+    collected(4, nrm2)
+
+    ready(4)
+    normed = nrm2[...].reshape(rows, width)
+    depth = width // n_grp
+    total = None
+    for s in range(n_grp):
+        term = mm(normed[:, s * depth:(s + 1) * depth], up_v[s])
+        total = term if total is None else total + term
+    hid[...] = gelu_exact(total).astype(jnp.bfloat16)
+    forward(5)
+    ready(5)
+    branch_out(2, hid[...], down_v)
+    stream = summed(2, stream)
+
+    back[...] = stream.reshape(n_grp, loc, width)
+    fin[i, g] = back[g]
+    for d in range(1, n_grp):
+        to = peer(g, n_grp, d)
+        remote(back.at[to], fin.at[i, g], tsend.at[1, d], trecv.at[1, g], "grp", to)
+    for d in range(1, n_grp):
+        src = peer(g, n_grp, d)
+        arrived(fin.at[i, src], tsend.at[1, d], trecv.at[1, src], "grp", src)
+    spread(6, lambda to: fin.at[i], fin)
+    head_copy.wait()
+    collected(6, fin)
+    out[0] = mm(fin[...].reshape(rows, width), head_v[...]).astype(jnp.bfloat16)
+    for copy in started:
+        copy.wait_send()
+
+
+def local_fused(mesh, patches, embed_kernel, location_embed, attn_in, attn_out, ffn_up, ffn_down, head_kernel):
+    n_rep, n_grp, n_img = mesh.shape["rep"], mesh.shape["grp"], mesh.shape["img"]
+    _, rows, p_size = patches.shape
+    share = embed_kernel.shape[2]
+    width = share * n_img
+    loc_count = location_embed.shape[0]
+    own = rows // n_img
+    heads_w = attn_in.shape[3]
+    depth = attn_in.shape[1]
+    hidden = ffn_up.shape[1]
+    recon_w = head_kernel.shape[2]
+    place = own // n_grp
+    w_in = attn_in.transpose(0, 2, 1, 3)
+    bf = jnp.bfloat16
+    dims = (n_rep, n_grp, n_img, rows, width)
+    vm = lambda *s: pltpu.VMEM(s, bf)
+    sem = lambda *s: pltpu.SemaphoreType.DMA(s)
+    return pl.pallas_call(
+        functools.partial(fused, dims),
+        out_shape=jax.ShapeDtypeStruct((1, rows, recon_w), bf),
+        in_specs=[pl.BlockSpec(memory_space=pl.ANY)] * 9,
+        out_specs=pl.BlockSpec(memory_space=pltpu.VMEM),
+        scratch_shapes=[
+            vm(rows, p_size), vm(p_size, share), vm(loc_count, share), vm(width, recon_w),
+            vm(n_grp, 3, depth, heads_w), vm(n_grp, 3, depth, heads_w),
+            vm(n_grp, heads_w, depth), vm(n_grp, heads_w, depth),
+            vm(n_grp, depth, hidden), vm(n_grp, hidden, depth),
+            vm(n_img, rows, share), vm(rows, width), vm(n_img, own, width), vm(n_img, own, width),
+            vm(3, rows, width), vm(3, n_img, own, width), vm(2, own, width),
+            vm(n_grp, place, width), vm(n_grp, place, width), vm(n_img, n_grp, place, width),
+            vm(rows, hidden),
+            sem(6, n_grp), sem(6, n_grp), sem(6, n_grp), sem(6, n_grp),
+            sem(7, n_img), sem(7, n_img), sem(2, n_grp), sem(2, n_grp),
+            sem(10), pltpu.SemaphoreType.REGULAR,
+        ],
+        compiler_params=pltpu.CompilerParams(
+            collective_id=0, has_side_effects=True, vmem_limit_bytes=48 * 1024 * 1024
+        ),
+    )(patches, embed_kernel, location_embed, w_in[0], w_in[1], attn_out, ffn_up, ffn_down, head_kernel)
+
+
+def fits(mesh, rows):
+    return mesh.shape["rep"] == 2 and rows % (mesh.shape["grp"] * mesh.shape["img"] * 16) == 0
+
+
+def serve(mesh, patches, *weights):
+    loc_count = weights[1].shape[0]
+    rows = patches.shape[1]
+    if fits(mesh, rows) and rows // loc_count == mesh.shape["img"]:
+        return local_fused(mesh, patches, *weights)
+    return local(patches, *weights)
+
+
 def solution(mesh):
     return jax.shard_map(
-        local,
+        functools.partial(serve, mesh),
         mesh=mesh,
         in_specs=(
             P("grp", "rep", None),

time: 359 us -> 177 us (0.49)
  waiting for transfers between devices: 201 us -> 0 us
  Pallas kernels: 0 us -> 170 us
  blocking collectives: 92.2 us -> 0 us
  matrix products: 23.6 us -> 0 us
  between operations: 13.8 us -> 0.03 us
  other arithmetic: 8.73 us -> 0 us
  local copies, waits for them, and re-layouts: 11.7 us -> 6.51 us
  starting transfers between devices: 5.07 us -> 0 us
    pallas_call x0 -> x1, Pallas kernels: none -> 170 us  [local_fused(): pl.pallas_call(functools.partial(fused, dims), out_shape=jax.ShapeDtypeSt...]
    all_gather x4 -> x0, waiting for transfers between devices: 113 us -> none  [the longest x1 46.9 us: local(): lax.all_gather(ffn_down, 'grp', axis=1, tiled=True)]
    psum x3 -> x0, waiting for transfers between devices: 87.4 us -> none  [add_branch(): total = lax.psum(branch.astype(jnp.bfloat16), 'img').astype(jnp.float32)]
    all_gather x3 -> x0, blocking collectives: 74 us -> none  [the longest x2 65.5 us: fetch(): lax.all_gather(attn_out[index], 'grp', axis=1, tiled=True)]
    dot_general x10 -> x0, matrix products: 21.4 us -> none  [the longest x1 6.55 us: feed_forward(): branch = jnp.dot(inner, w_down, preferred_element_type=jnp.float32)]
    all_to_all x1 -> x0, blocking collectives: 18.3 us -> none  [local(): lax.all_to_all(placed.reshape(groups, per_group, width), 'grp', split_axi...]
    all_to_all x1 -> x0, starting transfers between devices: 4.87 us -> none  [local(): lax.all_to_all(stream.reshape(1, rows, width), 'grp', split_axis=1, conca...]
    unnamed x1 -> x0, other arithmetic: 3.69 us -> none
  transfers between devices with their start and end apart: 8 -> 0, of which waited for: 7 -> 0; matrix products, arithmetic and copies ran while one was open for 4% -> 0% of each run, Pallas kernels for 0% -> 0%
where the time goes in v1:
time: 177 us; the launch traced here: 176 us
  Pallas kernels  170 us (96%)
  local copies, waits for them, and re-layouts  6.51 us (4%)
    pallas_call x1, Pallas kernels, local_fused(): pl.pallas_call(functools.partial(fused, dims), out_shape=jax.ShapeDtypeSt...  170 us
    unnamed x13, local copies, waits for them, and re-layouts  5.23 us

profile of v1, /device:TPU:1, one launch (start us, length us, event | category | flops | bytes accessed | tf_op | source)
XLA Modules:
  0.0 176.4 jit_solution(11109284388419409264)
XLA Ops:
  0.0 0.0 copy-start.4
  0.0 0.0 copy-start
  0.0 1.3 slice_bitcast_fusion
  1.3 0.0 copy-done.4
  1.3 0.3 copy-done
  1.6 0.0 copy-start.1
  1.6 1.3 copy-done.1
  3.0 0.0 copy-start.2
  3.0 1.0 copy-done.2
  4.0 0.0 copy-start.3
  4.0 1.0 copy-done.3
  5.0 0.0 copy-start.5
  5.0 0.8 copy-done.5
  5.8 169.9 %shard_map.82 = bf16[1,256,640]{2,1,0:T(8,128)(2,1)S(1)} custom-call(bf16[1,256,2560]{2,1,0:T(8,128)(2,1)S(1)} %copy-done, bf16[1,2560,256]{2,1,0:T(8,128)(2,1)S(1)} %copy-done.1, bf16[64,256]{1,0:T(8,128)(2,1)S(1)} %copy-done.5, bf16[3,256,256]{2,1,0:T(8,128)(2,1)S(1)} %get-tuple-element.6.w_in0, bf16[3,256,256]{2,1,0:T(8,128)(2,1)S(1)} %get-tuple-element.5.w_in1, ...), custom_call_target="tpu_custom_call" | custom-call | tf_op jit(solution)/shard_map/pallas_call | solution.py:396
  175.7 0.7 copy.10
Async XLA Ops:
  0.0 1.3 copy-start.4
  0.0 1.6 copy-start
  1.6 1.3 copy-start.1
  3.0 1.0 copy-start.2
  4.0 1.0 copy-start.3
  5.0 0.8 copy-start.5

commit v2 on v1

--- a/solution.py
+++ b/solution.py
@@ -10,6 +10,8 @@
 
 HD = 64
 MESH = pl.DeviceIdType.MESH
+SPLIT = (4, 1, 4, 1, 4, 4)
+WINDOW = 3
 
 
 def norm_rows(stream):
@@ -147,7 +149,7 @@
     patches_v, embed_v, loc_v, head_v,
     win0, win1, wout0, wout1, up_v, down_v,
     feats, nrm0, nrm1, nrm2, part, rs, keep, a2a, back, fin, hid,
-    zsend, zrecv, ysend, yrecv, xsend, xrecv, tsend, trecv, lsem, barrier_pad,
+    zsend, zrecv, ysend, yrecv, xsend, xrecv, tsend, trecv, lsem,
 ):
     n_rep, n_grp, n_img, rows, width = dims
     own = rows // n_img
@@ -166,7 +168,7 @@
                 barrier, inc=1, device_id={axis: peer(me, n, d)}, device_id_type=MESH
             )
 
-    started = []
+    started, guarded = [], []
 
     def remote(src, dst, send, recv, axis, to):
         copy = pltpu.make_async_remote_copy(
@@ -182,22 +184,17 @@
             device_id={axis: to}, device_id_type=MESH,
         ).wait_recv()
 
-    def cut1(ref, half):
-        size = ref.shape[0] // n_rep
-        return ref.at[pl.ds(pl.multiple_of(half * size, size), size)]
-
-    def cut2(ref, half):
-        size = ref.shape[1] // n_rep
-        return ref.at[:, pl.ds(pl.multiple_of(half * size, size), size)]
-
-    weights = (
-        (w_in0, win0, cut2),
-        (w_out.at[0], wout0, cut1),
-        (w_in1, win1, cut2),
-        (w_out.at[1], wout1, cut1),
-        (up, up_v, cut1),
-        (down, down_v, cut1),
-    )
+    tensors = ((w_in0, win0), (w_out.at[0], wout0), (w_in1, win1), (w_out.at[1], wout1), (up, up_v), (down, down_v))
+    pieces = []
+    for t, count in enumerate(SPLIT):
+        pieces += [(t, count, at) for at in range(count)]
+
+    def cut(t, count, at, ref, half):
+        axis = 1 if t in (0, 2) else 0
+        size = ref.shape[axis] // (n_rep * count)
+        rows_at = pl.ds(pl.multiple_of((half * count + at) * size, size), size)
+        return ref.at[:, rows_at] if axis else ref.at[rows_at]
+
     locals_ = []
 
     def local_copy(src, dst):
@@ -206,41 +203,88 @@
         locals_.append(copy)
         return copy
 
+    last = n_grp - 1
+
+    def remote_if(cond, src, dst, send, recv, to):
+        copy = pltpu.make_async_remote_copy(
+            src_ref=src, dst_ref=dst, send_sem=send, recv_sem=recv,
+            device_id={"grp": to}, device_id_type=MESH,
+        )
+        pl.when(cond)(copy.start)
+        guarded.append((cond, copy))
+
     def start_z(k):
-        shard, full, cut = weights[k]
-        for d in range(1, n_grp):
-            remote(
-                cut(shard, y), cut(full.at[g], y),
-                zsend.at[k, d], zrecv.at[k, g], "grp", peer(g, n_grp, d),
+        t, count, at = pieces[k]
+        shard, full = tensors[t]
+        for d in (2, -2, 1, -1):
+            to = g + d
+            inside = jnp.logical_and(to >= 0, to <= last)
+            to = lax.min(lax.max(to, 0), last)
+            remote_if(
+                inside, cut(t, count, at, shard, y), cut(t, count, at, full.at[g], y),
+                zsend.at[k, d + 2], zrecv.at[k, g], to,
             )
 
-    def forward(k, hops=None):
-        shard, full, cut = weights[k]
-        for d in hops or range(1, n_grp):
-            src = peer(g, n_grp, d)
-            arrived(cut(full.at[src], y), zsend.at[k, d], zrecv.at[k, src], "grp", src)
-            remote(
-                cut(full.at[src], y), cut(full.at[src], y),
-                ysend.at[k, d], yrecv.at[k, src], "rep", peer(y, n_rep, 1),
-            )
-
-    def ready(k):
-        shard, full, cut = weights[k]
-        for d in range(1, n_grp):
-            src = peer(g, n_grp, d)
-            half = peer(y, n_rep, 1)
-            arrived(cut(full.at[src], half), ysend.at[k, d], yrecv.at[k, src], "rep", half)
-        own_copies[k].wait()
-
-    def spread(k, src_of, dst):
-        for d in range(1, n_img):
-            to = peer(i, n_img, d)
-            remote(src_of(to), dst.at[i], xsend.at[k, d], xrecv.at[k, i], "img", to)
+    def forward(k):
+        if k + WINDOW < len(pieces):
+            start_z(k + WINDOW)
+        t, count, at = pieces[k]
+        shard, full = tensors[t]
+        inner = jnp.logical_and(g > 0, g < last)
+        low = g < n_grp // 2
+        order = (
+            jnp.where(g == 0, 1, jnp.where(g == last, last - 1, jnp.where(low, 0, last))),
+            jnp.where(g == 0, 2, jnp.where(g == last, last - 2, jnp.where(low, g + 1, g - 1))),
+            jnp.where(g == 0, last, jnp.where(g == last, 0, jnp.where(low, last, 0))),
+        )
+        for n, src in enumerate(order):
+            view = cut(t, count, at, full.at[src], y)
+            arrived(view, zsend.at[k, 0], zrecv.at[k, src], "grp", src)
+            if n == 2:
+                outer = jnp.where(low, 0, last)
+                away = jnp.where(outer == g, jnp.where(low, 1, last - 1), outer)
+                remote_if(inner, view, view, zsend.at[k, 2], zrecv.at[k, src], away)
+            remote(view, view, ysend.at[k, n], yrecv.at[k, src], "rep", peer(y, n_rep, 1))
+
+    done = []
+
+    def pump(t, share):
+        upto = sum(SPLIT[:t]) + int(SPLIT[t] * share)
+        while len(done) < upto:
+            forward(len(done))
+            done.append(1)
+
+    def ready(t):
+        half = peer(y, n_rep, 1)
+        shard, full = tensors[t]
+        for k, (of, count, at) in enumerate(pieces):
+            if of == t:
+                for d in range(1, n_grp):
+                    src = peer(g, n_grp, d)
+                    arrived(cut(t, count, at, full.at[src], half), ysend.at[k, d], yrecv.at[k, src], "rep", half)
+        own_copies[t].wait()
+
+    sibling = i + 1 - 2 * lax.rem(i, 2)
+    across = lax.rem(i + 2, n_img)
+    beyond = lax.rem(sibling + 2, n_img)
+
+    def halves(ref):
+        size = ref.shape[0] // 2
+        return (ref.at[pl.ds(0, size)], ref.at[pl.ds(size, size)])
+
+    def spread(k, dst):
+        for h, view in enumerate(halves(dst.at[i])):
+            remote(view, view, xsend.at[k, 0, h], xrecv.at[k, i, h], "img", across)
+        for h, view in enumerate(halves(dst.at[i])):
+            remote(view, view, xsend.at[k, 1, h], xrecv.at[k, i, h], "img", sibling)
 
     def collected(k, dst):
-        for d in range(1, n_img):
-            src = peer(i, n_img, d)
-            arrived(dst.at[src], xsend.at[k, d], xrecv.at[k, src], "img", src)
+        for h, view in enumerate(halves(dst.at[across])):
+            arrived(view, xsend.at[k, 0, h], xrecv.at[k, across, h], "img", across)
+            remote(view, view, xsend.at[k, 2, h], xrecv.at[k, across, h], "img", sibling)
+        for src in (sibling, beyond):
+            for h, view in enumerate(halves(dst.at[src])):
+                arrived(view, xsend.at[k, 1, h], xrecv.at[k, src, h], "img", sibling)
 
     in_copies = [
         local_copy(patches.at[0], patches_v),
@@ -248,9 +292,9 @@
         local_copy(loc_in, loc_v),
     ]
     pl.semaphore_wait(barrier, n_grp + n_img + n_rep - 3)
-    start_z(0)
-    start_z(1)
-    own_copies = [local_copy(shard, full.at[g]) for shard, full, cut in weights]
+    for k in range(WINDOW):
+        start_z(k)
+    own_copies = [local_copy(shard, full.at[g]) for shard, full in tensors]
     head_copy = local_copy(head.at[0], head_v)
 
     for copy in in_copies:
@@ -260,8 +304,7 @@
     images = rows // places.shape[0]
     hidden = hidden.reshape(images, places.shape[0], hidden.shape[1]) + places[None]
     feats[i] = hidden.reshape(rows, hidden.shape[2]).astype(jnp.bfloat16)
-    spread(0, lambda to: feats.at[i], feats)
-    start_z(2)
+    spread(0, feats)
     collected(0, feats)
 
     chunk = width // n_img
@@ -275,10 +318,8 @@
     mine = pl.ds(pl.multiple_of(i * own, own), own)
     for s in range(n_img):
         keep[0, :, s * chunk:(s + 1) * chunk] = feats[s, mine, :]
-    forward(0)
-    start_z(3)
-    forward(1)
-    start_z(4)
+
+    pump(0, 1)
 
     row_at = lax.broadcasted_iota(jnp.int32, (rows, rows), 0)
     col_at = lax.broadcasted_iota(jnp.int32, (rows, rows), 1)
@@ -298,24 +339,35 @@
         wide = width // n_grp
         for s in range(n_grp):
             part[k, :, s * wide:(s + 1) * wide] = mm(mixed, full[s]).astype(jnp.bfloat16)
-        spread(
-            1 + 2 * k,
-            lambda to: part.at[k, pl.ds(pl.multiple_of(to * own, own), own)],
-            rs.at[k],
-        )
+        def rows_of(device):
+            return pl.ds(pl.multiple_of(device * own, own), own)
+
+        m = 1 + 2 * k
+        for slot, to in ((0, beyond), (1, sibling)):
+            remote(
+                part.at[k, rows_of(to)], rs.at[k, slot],
+                xsend.at[m, slot, 0], xrecv.at[m, slot, 0], "img", sibling,
+            )
+        arrived(rs.at[k, 0], xsend.at[m, 0, 0], xrecv.at[m, 0, 0], "img", sibling)
+        pair = part[k, rows_of(across), :].astype(jnp.float32) + rs[k, 0].astype(jnp.float32)
+        rs[k, 3] = pair.astype(jnp.bfloat16)
+        remote(rs.at[k, 3], rs.at[k, 2], xsend.at[m, 2, 0], xrecv.at[m, 2, 0], "img", across)
 
     def summed(k, stream):
+        m = 1 + 2 * k
         total = part[k, mine, :].astype(jnp.float32)
-        collected(1 + 2 * k, rs.at[k])
-        for d in range(1, n_img):
-            total = total + rs[k, peer(i, n_img, d)].astype(jnp.float32)
+        for slot, src in ((1, sibling), (2, across)):
+            arrived(rs.at[k, slot], xsend.at[m, slot, 0], xrecv.at[m, slot, 0], "img", src)
+            total = total + rs[k, slot].astype(jnp.float32)
         return (stream.astype(jnp.float32) + total).astype(jnp.bfloat16)
 
     ready(0)
     query, keys, values = project(nrm0[...], win0)
     mixed = head_attention(query, keys, values, same_image)
+    pump(1, 1)
     ready(1)
     branch_out(0, mixed, wout0)
+    pump(2, 0.5)
     keep[1] = summed(0, keep[0])
 
     for d in range(1, n_grp):
@@ -325,26 +377,26 @@
             tsend.at[0, d], trecv.at[0, g], "grp", to,
         )
     a2a[g] = keep[1, pl.ds(pl.multiple_of(g * loc, loc), loc), :]
-    start_z(5)
     for d in range(1, n_grp):
         src = peer(g, n_grp, d)
         arrived(a2a.at[src], tsend.at[0, d], trecv.at[0, src], "grp", src)
     stream = a2a[...].reshape(own, width)
     nrm1[i] = normalise(stream.astype(jnp.float32))
-    spread(2, lambda to: nrm1.at[i], nrm1)
-    forward(2)
-    forward(3)
+    spread(2, nrm1)
+    pump(2, 1)
     collected(2, nrm1)
 
     ready(2)
     query, keys, values = project(nrm1[...].reshape(rows, width), win1)
+    pump(3, 1)
     mixed = head_attention(query, keys, values, same_place)
     ready(3)
     branch_out(1, mixed, wout1)
+    pump(4, 0.5)
     stream = summed(1, stream)
     nrm2[i] = normalise(stream.astype(jnp.float32))
-    spread(4, lambda to: nrm2.at[i], nrm2)
-    forward(4)
+    spread(4, nrm2)
+    pump(4, 1)
     collected(4, nrm2)
 
     ready(4)
@@ -355,7 +407,7 @@
         term = mm(normed[:, s * depth:(s + 1) * depth], up_v[s])
         total = term if total is None else total + term
     hid[...] = gelu_exact(total).astype(jnp.bfloat16)
-    forward(5)
+    pump(5, 1)
     ready(5)
     branch_out(2, hid[...], down_v)
     stream = summed(2, stream)
@@ -368,12 +420,14 @@
     for d in range(1, n_grp):
         src = peer(g, n_grp, d)
         arrived(fin.at[i, src], tsend.at[1, d], trecv.at[1, src], "grp", src)
-    spread(6, lambda to: fin.at[i], fin)
+    spread(6, fin)
     head_copy.wait()
     collected(6, fin)
     out[0] = mm(fin[...].reshape(rows, width), head_v[...]).astype(jnp.bfloat16)
     for copy in started:
         copy.wait_send()
+    for cond, copy in guarded:
+        pl.when(cond)(copy.wait_send)
 
 
 def local_fused(mesh, patches, embed_kernel, location_embed, attn_in, attn_out, ffn_up, ffn_down, head_kernel):
@@ -407,18 +461,18 @@
             vm(3, rows, width), vm(3, n_img, own, width), vm(2, own, width),
             vm(n_grp, place, width), vm(n_grp, place, width), vm(n_img, n_grp, place, width),
             vm(rows, hidden),
-            sem(6, n_grp), sem(6, n_grp), sem(6, n_grp), sem(6, n_grp),
-            sem(7, n_img), sem(7, n_img), sem(2, n_grp), sem(2, n_grp),
-            sem(10), pltpu.SemaphoreType.REGULAR,
+            sem(sum(SPLIT), n_grp + 1), sem(sum(SPLIT), n_grp), sem(sum(SPLIT), n_grp), sem(sum(SPLIT), n_grp),
+            sem(7, n_img, 2), sem(7, n_img, 2), sem(2, n_grp), sem(2, n_grp),
+            sem(10),
         ],
         compiler_params=pltpu.CompilerParams(
-            collective_id=0, has_side_effects=True, vmem_limit_bytes=48 * 1024 * 1024
+            collective_id=0, has_side_effects=True, vmem_limit_bytes=60 * 1024 * 1024
         ),
     )(patches, embed_kernel, location_embed, w_in[0], w_in[1], attn_out, ffn_up, ffn_down, head_kernel)
 
 
 def fits(mesh, rows):
-    return mesh.shape["rep"] == 2 and rows % (mesh.shape["grp"] * mesh.shape["img"] * 16) == 0
+    return mesh.shape["rep"] == 2 and mesh.shape["grp"] == 4 and mesh.shape["img"] == 4 and rows % (mesh.shape["grp"] * mesh.shape["img"] * 16) == 0
 
 
 def serve(mesh, patches, *weights):

time: 177 us -> 133 us (0.75)
  Pallas kernels: 170 us -> 129 us
  local copies, waits for them, and re-layouts: 6.51 us -> 3.77 us
    pallas_call x1, Pallas kernels: 170 us -> 129 us  [local_fused(): pl.pallas_call(functools.partial(fused, dims), out_shape=jax.ShapeDtypeSt...]
    unnamed x13 -> x1, local copies, waits for them, and re-layouts: 5.23 us -> 1.73 us
where the time goes in v2:
time: 133 us
  Pallas kernels  129 us (97%)
  local copies, waits for them, and re-layouts  3.77 us (3%)
    pallas_call x1, Pallas kernels, local_fused(): pl.pallas_call(functools.partial(fused, dims), out_shape=jax.ShapeDtypeSt...  129 us

profile of v2, /device:TPU:1, one launch (start us, length us, event | category | flops | bytes accessed | tf_op | source)
XLA Modules:
  0.0 132.7 jit_solution(14016579644541661849)
XLA Ops:
  0.0 2.0 %slice_bitcast_fusion = (bf16[3,256,256]{2,1,0:T(8,128)(2,1)}, bf16[3,256,256]{2,1,0:T(8,128)(2,1)}) fusion(bf16[2,3,256,256]{3,2,1,0:T(8,128)(2,1)} %bitcast.5), kind=kLoop, calls=%fused_computation | loop fusion | bytes 1572864 | tf_op jit(solution)/shard_map/squeeze | solution.py:471
  2.0 128.9 %shard_map.82 = bf16[1,256,640]{2,1,0:T(8,128)(2,1)} custom-call(bf16[1,256,2560]{2,1,0:T(8,128)(2,1)} %patches.1, bf16[1,2560,256]{2,1,0:T(8,128)(2,1)} %embed.1, bf16[64,256]{1,0:T(8,128)(2,1)} %loc_in.1, bf16[3,256,256]{2,1,0:T(8,128)(2,1)} %get-tuple-element.6.w_in0, bf16[3,256,256]{2,1,0:T(8,128)(2,1)} %get-tuple-element.5.w_in1, ...), custom_call_target="tpu_custom_call" | custom-call | tf_op jit(solution)/shard_map/pallas_call | solution.py:450
  131.0 1.7 %copy.10 = bf16[1,256,640]{2,1,0:T(8,128)(2,1)} copy(bf16[1,256,640]{2,1,0:T(8,128)(2,1)} %shard_map.82) | data formatting | bytes 655360

commit v3 on v2

--- a/solution.py
+++ b/solution.py
@@ -10,7 +10,7 @@
 
 HD = 64
 MESH = pl.DeviceIdType.MESH
-SPLIT = (4, 1, 4, 1, 4, 4)
+SPLIT = (4, 2, 4, 2, 4, 8)
 WINDOW = 3
 
 
@@ -225,34 +225,42 @@
                 zsend.at[k, d + 2], zrecv.at[k, g], to,
             )
 
-    def forward(k):
-        if k + WINDOW < len(pieces):
+    def forward(k, hops=(0, 1, 2)):
+        if 0 in hops and k + WINDOW < len(pieces):
             start_z(k + WINDOW)
         t, count, at = pieces[k]
         shard, full = tensors[t]
         inner = jnp.logical_and(g > 0, g < last)
         low = g < n_grp // 2
+        far = jnp.where(low, last, 0)
         order = (
-            jnp.where(g == 0, 1, jnp.where(g == last, last - 1, jnp.where(low, 0, last))),
+            jnp.where(g == 0, 1, jnp.where(g == last, last - 1, far)),
             jnp.where(g == 0, 2, jnp.where(g == last, last - 2, jnp.where(low, g + 1, g - 1))),
-            jnp.where(g == 0, last, jnp.where(g == last, 0, jnp.where(low, last, 0))),
+            jnp.where(inner, jnp.where(low, 0, last), far),
         )
-        for n, src in enumerate(order):
+        for n in hops:
+            src = order[n]
             view = cut(t, count, at, full.at[src], y)
             arrived(view, zsend.at[k, 0], zrecv.at[k, src], "grp", src)
-            if n == 2:
+            if n == 0:
                 outer = jnp.where(low, 0, last)
                 away = jnp.where(outer == g, jnp.where(low, 1, last - 1), outer)
                 remote_if(inner, view, view, zsend.at[k, 2], zrecv.at[k, src], away)
             remote(view, view, ysend.at[k, n], yrecv.at[k, src], "rep", peer(y, n_rep, 1))
 
-    done = []
+    done, late = [], [0]
 
     def pump(t, share):
         upto = sum(SPLIT[:t]) + int(SPLIT[t] * share)
         while len(done) < upto:
-            forward(len(done))
+            forward(len(done), (0, 1))
+            if len(done) > late[0]:
+                forward(late[0], (2,))
+                late[0] += 1
             done.append(1)
+        if share == 1 and late[0] < len(done):
+            forward(late[0], (2,))
+            late[0] += 1
 
     def ready(t):
         half = peer(y, n_rep, 1)
@@ -367,7 +375,7 @@
     pump(1, 1)
     ready(1)
     branch_out(0, mixed, wout0)
-    pump(2, 0.5)
+    pump(2, 0.25)
     keep[1] = summed(0, keep[0])
 
     for d in range(1, n_grp):
@@ -376,6 +384,7 @@
             keep.at[1, pl.ds(pl.multiple_of(to * loc, loc), loc)], a2a.at[g],
             tsend.at[0, d], trecv.at[0, g], "grp", to,
         )
+    pump(2, 0.5)
     a2a[g] = keep[1, pl.ds(pl.multiple_of(g * loc, loc), loc), :]
     for d in range(1, n_grp):
         src = peer(g, n_grp, d)
@@ -385,6 +394,7 @@
     spread(2, nrm1)
     pump(2, 1)
     collected(2, nrm1)
+    pump(3, 1)
 
     ready(2)
     query, keys, values = project(nrm1[...].reshape(rows, width), win1)
@@ -392,12 +402,15 @@
     mixed = head_attention(query, keys, values, same_place)
     ready(3)
     branch_out(1, mixed, wout1)
+    pump(4, 0.25)
+    stream = summed(1, stream)
     pump(4, 0.5)
-    stream = summed(1, stream)
     nrm2[i] = normalise(stream.astype(jnp.float32))
     spread(4, nrm2)
     pump(4, 1)
+    pump(5, 0.125)
     collected(4, nrm2)
+    pump(5, 0.25)
 
     ready(4)
     normed = nrm2[...].reshape(rows, width)

time: 133 us -> 130 us (0.977)
  Pallas kernels: 129 us -> 126 us
    pallas_call x1, Pallas kernels: 129 us -> 126 us  [local_fused(): pl.pallas_call(functools.partial(fused, dims), out_shape=jax.ShapeDtypeSt...]
where the time goes in v3:
time: 130 us; the launch traced here: 129 us
  Pallas kernels  126 us (97%)
  local copies, waits for them, and re-layouts  3.77 us (3%)
    pallas_call x1, Pallas kernels, local_fused(): pl.pallas_call(functools.partial(fused, dims), out_shape=jax.ShapeDtypeSt...  126 us

profile of v3, /device:TPU:1, one launch (start us, length us, event | category | flops | bytes accessed | tf_op | source)
XLA Modules:
  0.0 129.4 jit_solution(5628824424696768654)
XLA Ops:
  0.0 2.0 %slice_bitcast_fusion = (bf16[3,256,256]{2,1,0:T(8,128)(2,1)}, bf16[3,256,256]{2,1,0:T(8,128)(2,1)}) fusion(bf16[2,3,256,256]{3,2,1,0:T(8,128)(2,1)} %bitcast.5), kind=kLoop, calls=%fused_computation | loop fusion | bytes 1572864 | tf_op jit(solution)/shard_map/squeeze | solution.py:484
  2.0 125.6 %shard_map.82 = bf16[1,256,640]{2,1,0:T(8,128)(2,1)} custom-call(bf16[1,256,2560]{2,1,0:T(8,128)(2,1)} %patches.1, bf16[1,2560,256]{2,1,0:T(8,128)(2,1)} %embed.1, bf16[64,256]{1,0:T(8,128)(2,1)} %loc_in.1, bf16[3,256,256]{2,1,0:T(8,128)(2,1)} %get-tuple-element.6.w_in0, bf16[3,256,256]{2,1,0:T(8,128)(2,1)} %get-tuple-element.5.w_in1, ...), custom_call_target="tpu_custom_call" | custom-call | tf_op jit(solution)/shard_map/pallas_call | solution.py:463
  127.7 1.7 %copy.10 = bf16[1,256,640]{2,1,0:T(8,128)(2,1)} copy(bf16[1,256,640]{2,1,0:T(8,128)(2,1)} %shard_map.82) | data formatting | bytes 655360
